TPU v7x, 32 devices: a whole 2x2x4 slice. The times are simulated.
32 devices in a mesh: grp: 2 (over x), leaf: 8 (over z, y), sub: 2 (over core).
Axes of the slice: x: 2, y: 2, z: 4, core: 2. Of those that a mesh axis runs over, the one named last changes fastest.
Arguments:
- right_side: float32 [512, 2048], P(('grp', 'leaf', 'sub')), parts along dimension 0, may hold values from -24 to 24, as said below
- first_guess: float32 [512, 2048], P(('grp', 'leaf', 'sub')), parts along dimension 0, may hold values from -3 to 3
- couple: bfloat16 [512, 64, 384], P(('grp', 'leaf', 'sub')), parts along dimension 0, may hold values from -0.75 to 0.75
- send_lists: int32 [32, 2, 4], P(('grp', 'leaf', 'sub')), parts along dimension 0, may hold values from -1 to 15, as said below
- neighbours: int32 [512, 6], P(('grp', 'leaf', 'sub')), parts along dimension 0, may hold values from -1 to 23, as said below
Outputs:
- solution: float32 [512, 2048], P(('grp', 'leaf', 'sub')), parts along dimension 0
- residual: float32 [512, 2048], P(('grp', 'leaf', 'sub')), parts along dimension 0
There are 2 independent parts, one for each index of `grp`. A program takes and returns all parts, laid end to end along the dimension named above; each array names one. Nothing has to cross between parts.
Inputs may be any that keep to these rules, and one draw needn't show every extreme that they name: `right_side`: rows rise in scale along the element order. `send_lists`: for device d of a part and direction 0 (toward device d + 1) or 1 (toward device d - 1): distinct local element indices in the live slots, which come first, and -1 after them. The first device sends nothing in direction 1, the last nothing in direction 0; some device fills all 4 slots in direction 0 and the device after it all 4 in direction 1. `neighbours`: positions below 16 are the device's own elements, 16 + s the live slot s received from the previous device, 20 + s the live slot s received from the next device; -1 marks a face on the band's boundary.
All inputs are finite; a program needn't handle non-finite values.
Results may differ from a plain program's by a relative error of at most 0.034.
Values may be sent and summed in bfloat16 or wider, within the bound.
A program may use at most 64 MiB of HBM per device.

v0:
```python
import jax
import jax.numpy as jnp
from jax import lax
from jax.sharding import PartitionSpec as P

DOF = 64
FACES = 6
RHS = 32
SSTEP = 3
CYCLES = 4


def from_behind(value, axis, steps):
    count = lax.axis_size(axis)
    first, last = (max(0, -steps), min(count, count - steps))
    return lax.ppermute(value, axis, [(source, source + steps) for source in range(first, last)])


def couple_apply(vector_field, couple, send_lists, neighbours):
    local_count = vector_field.shape[0]
    slot_count = send_lists.shape[2]
    row_width = vector_field.shape[1]
    halves = vector_field.astype(jnp.bfloat16)
    own_lists = send_lists[0]
    chosen = jnp.take(halves, jnp.maximum(own_lists, 0).reshape(-1), axis=0).reshape(
        2, slot_count, row_width
    )
    chosen = jnp.where(own_lists[:, :, None] >= 0, chosen, jnp.zeros_like(chosen))
    forward = chosen[0]
    backward = chosen[1]
    before_blocks = from_behind(forward, ("leaf", "sub"), 1)
    after_blocks = from_behind(backward, ("leaf", "sub"), -1)
    zero_block = jnp.zeros((1, row_width), jnp.bfloat16)
    extended = jnp.concatenate([halves, before_blocks, after_blocks, zero_block], axis=0)
    positions = jnp.where(neighbours < 0, local_count + 2 * slot_count, neighbours).reshape(-1)
    gathered = jnp.take(extended, positions, axis=0).reshape(local_count, FACES * DOF, RHS)
    product = jnp.einsum("eik,ekr->eir", couple, gathered, preferred_element_type=jnp.float32)
    return product.reshape(local_count, DOF * RHS)


def to_columns(vector_field):
    return vector_field.reshape(-1, RHS)


def basis_sums(stacked):
    partial_sum = jnp.dot(
        stacked.T, stacked, precision=lax.Precision.HIGHEST, preferred_element_type=jnp.float32
    )
    total_sum = lax.psum(partial_sum, ("leaf", "sub"))
    return (total_sum[: SSTEP * RHS, : SSTEP * RHS], total_sum[: SSTEP * RHS, SSTEP * RHS :])


def shards(right_side, first_guess, couple, send_lists, neighbours):
    solution = first_guess
    residual = right_side - first_guess + couple_apply(first_guess, couple, send_lists, neighbours)
    for repeat in range(CYCLES):
        krylov_blocks = [residual]
        for degree in range(SSTEP):
            krylov_blocks.append(couple_apply(krylov_blocks[-1], couple, send_lists, neighbours))
        images = [
            krylov_blocks[order_index] - krylov_blocks[order_index + 1]
            for order_index in range(SSTEP)
        ]
        stacked = jnp.concatenate(
            [to_columns(image_block) for image_block in images] + [to_columns(residual)], axis=1
        )
        square_block, right_block = basis_sums(stacked)
        factor = jnp.linalg.cholesky(square_block)
        coeffs = jax.scipy.linalg.cho_solve((factor, True), right_block)
        krylov = jnp.concatenate(
            [to_columns(basis_block) for basis_block in krylov_blocks[:SSTEP]], axis=1
        )
        solution = solution + jnp.dot(
            krylov, coeffs, precision=lax.Precision.HIGHEST, preferred_element_type=jnp.float32
        ).reshape(solution.shape)
        residual = residual - jnp.dot(
            stacked[:, : SSTEP * RHS],
            coeffs,
            precision=lax.Precision.HIGHEST,
            preferred_element_type=jnp.float32,
        ).reshape(residual.shape)
    return (solution, residual)


def solution(mesh):
    placed = (
        P(("grp", "leaf", "sub"), None),
        P(("grp", "leaf", "sub"), None),
        P(("grp", "leaf", "sub"), None, None),
        P(("grp", "leaf", "sub"), None, None),
        P(("grp", "leaf", "sub"), None),
    )
    return jax.shard_map(
        shards,
        mesh=mesh,
        in_specs=placed,
        out_specs=(P(("grp", "leaf", "sub"), None), P(("grp", "leaf", "sub"), None)),
        check_vma=False,
    )
```

profile of v0, /device:TPU:8, one launch (start us, length us, event | category | flops | bytes accessed | tf_op | source)
XLA Modules:
  0.0 679.5 jit_solution(5330621828256337347)
XLA Ops:
  10.5 1.9 collective-permute-start
  12.4 4.5 collective-permute-start.1
  22.6 2.6 collective-permute-start.2
  25.2 3.8 collective-permute-start.3
  29.1 1.4 collective-permute-done.3
  32.3 2.2 reshape.259
  37.1 2.5 collective-permute-start.4
  39.6 4.0 collective-permute-start.5
  43.5 1.4 collective-permute-done.5
  46.7 2.2 reshape.262
  51.0 2.5 collective-permute-start.6
  53.5 4.2 collective-permute-start.7
  62.2 2.2 reshape.265
  66.7 87.3 %all-reduce.5.cloned.1.call-done = f32[128,128]{0,1:T(8,128)} async-done(((f32[128,128]{0,1:T(8,128)}), f32[128,128]{0,1:T(8,128)}) %all-reduce.5.cloned.1.call-update) | async-done | bytes 65552 | tf_op jit(solution)/shard_map/psum | solution.py:49
  155.8 8.8 %cholesky.74 = f32[96,96]{1,0:T(8,128)S(1)} custom-call(f32[96,96]{1,0:T(8,128)S(1)} %fusion.103), custom_call_target="Cholesky" | custom-call | tf_op jit(solution)/shard_map/jit(cholesky)/cholesky | solution.py:68
  165.9 7.4 %custom-call.10 = f32[1,96,96]{1,2,0:T(8,128)S(1)} custom-call(f32[1,96,96]{2,1,0:T(8,128)S(1)} %fusion.80), custom_call_target="InvertDiagBlocksLowerTriangular" | custom-call | tf_op jit(solution)/shard_map/jit(_cho_solve)/triangular_solve | solution.py:69
  176.5 1.9 collective-permute-start.8
  178.5 4.5 collective-permute-start.9
  183.0 1.4 collective-permute-done.9
  189.5 1.9 collective-permute-start.10
  191.5 4.9 collective-permute-start.11
  199.4 2.2 reshape.274
  201.6 1.3 fusion.133
  207.1 1.9 collective-permute-start.12
  209.0 4.5 collective-permute-start.13
  219.4 2.2 reshape.277
  224.8 86.2 %all-reduce.7.cloned.1.call-done = f32[128,128]{0,1:T(8,128)} async-done(((f32[128,128]{0,1:T(8,128)}), f32[128,128]{0,1:T(8,128)}) %all-reduce.7.cloned.1.call-update) | async-done | bytes 65552 | tf_op jit(solution)/shard_map/psum | solution.py:49
  312.7 8.8 %cholesky.85 = f32[96,96]{1,0:T(8,128)S(1)} custom-call(f32[96,96]{1,0:T(8,128)S(1)} %fusion.98), custom_call_target="Cholesky" | custom-call | tf_op jit(solution)/shard_map/jit(cholesky)/cholesky | solution.py:68
  322.8 7.4 %custom-call.11 = f32[1,96,96]{1,2,0:T(8,128)S(1)} custom-call(f32[1,96,96]{2,1,0:T(8,128)S(1)} %fusion.81), custom_call_target="InvertDiagBlocksLowerTriangular" | custom-call | tf_op jit(solution)/shard_map/jit(_cho_solve)/triangular_solve | solution.py:69
  334.1 2.1 collective-permute-start.14
  336.2 4.5 collective-permute-start.15
  340.7 1.4 collective-permute-done.15
  344.1 2.2 reshape.283
  346.3 1.3 convolution_bitcast_fusion.5
  350.7 1.9 collective-permute-start.16
  352.6 4.5 collective-permute-start.17
  357.1 1.4 collective-permute-done.17
  360.5 2.2 reshape.286
  362.7 1.3 fusion.134
  368.2 1.9 collective-permute-start.18
  370.2 4.5 collective-permute-start.19
  380.9 2.2 reshape.289
  386.5 85.9 %all-reduce.9.cloned.1.call-done = f32[128,128]{0,1:T(8,128)} async-done(((f32[128,128]{0,1:T(8,128)}), f32[128,128]{0,1:T(8,128)}) %all-reduce.9.cloned.1.call-update) | async-done | bytes 65552 | tf_op jit(solution)/shard_map/psum | solution.py:49
  474.1 8.8 %cholesky.96 = f32[96,96]{1,0:T(8,128)S(1)} custom-call(f32[96,96]{1,0:T(8,128)S(1)} %fusion.93), custom_call_target="Cholesky" | custom-call | tf_op jit(solution)/shard_map/jit(cholesky)/cholesky | solution.py:68
  484.3 7.4 %custom-call.12 = f32[1,96,96]{1,2,0:T(8,128)S(1)} custom-call(f32[1,96,96]{2,1,0:T(8,128)S(1)} %fusion.82), custom_call_target="InvertDiagBlocksLowerTriangular" | custom-call | tf_op jit(solution)/shard_map/jit(_cho_solve)/triangular_solve | solution.py:69
  495.0 1.9 collective-permute-start.20
  496.9 4.5 collective-permute-start.21
  505.4 2.2 reshape.295
  507.7 1.3 convolution_bitcast_fusion.2
  511.1 1.7 fusion.124
  515.0 1.9 collective-permute-start.22
  517.0 4.9 collective-permute-start.23
  521.9 1.5 fusion
  523.5 1.9 reshape.267
  529.3 2.2 reshape.298
  531.6 1.3 fusion.135
  537.1 1.9 collective-permute-start.24
  539.1 4.5 collective-permute-start.25
  546.4 2.0 copy.147
  554.9 2.5 reshape.301
  560.1 2.2 fusion.48
  566.2 82.3 %all-reduce.11.cloned.1.call-done = f32[128,128]{0,1:T(8,128)} async-done(((f32[128,128]{0,1:T(8,128)}), f32[128,128]{0,1:T(8,128)}) %all-reduce.11.cloned.1.call-update) | async-done | bytes 65552 | tf_op jit(solution)/shard_map/psum | solution.py:49
  650.3 8.8 %cholesky.107 = f32[96,96]{1,0:T(8,128)S(1)} custom-call(f32[96,96]{1,0:T(8,128)S(1)} %fusion.88), custom_call_target="Cholesky" | custom-call | tf_op jit(solution)/shard_map/jit(cholesky)/cholesky | solution.py:68
  660.4 7.4 %custom-call.13 = f32[1,96,96]{1,2,0:T(8,128)S(1)} custom-call(f32[1,96,96]{2,1,0:T(8,128)S(1)} %fusion.83), custom_call_target="InvertDiagBlocksLowerTriangular" | custom-call | tf_op jit(solution)/shard_map/jit(_cho_solve)/triangular_solve | solution.py:69
  (444 shorter events, 123.9 us)
Async XLA Ops:
  7.2 13.5 %copy-start = (bf16[16,64,384]{2,1,0:T(8,128)(2,1)S(1)}, bf16[16,64,384]{2,1,0:T(8,128)(2,1)}, u32[]{:S(2)}) copy-start(bf16[16,64,384]{2,1,0:T(8,128)(2,1)} %param.14) | copy-start | bytes 2359300
  7.2 146.9 %all-reduce.5.cloned.1.call-start = ((), (), s32[]{:S(2)}) async-start(), calls=%async_computation | async-start | bytes 131072 | tf_op jit(solution)/shard_map/psum | solution.py:49
  8.0 42.9 %copy-start.57 = (pred[2,4]{1,0:T(4,128)(4,1)}, pred[2,4]{1,0:T(4,128)(4,1)S(1)}, u32[]{:S(2)}) copy-start(pred[2,4]{1,0:T(4,128)(4,1)S(1)} %compare_bitcast_fusion) | copy-start | bytes 28
  8.8 42.0 %copy-start.63 = (pred[8]{0:T(512)(128)(4,1)}, pred[8]{0:T(512)(128)(4,1)S(1)}, u32[]{:S(2)}) copy-start(pred[8]{0:T(512)(128)(4,1)S(1)} %compare_and_fusion.1) | copy-start | bytes 28
  8.8 27.5 %copy-start.78 = (s32[1024]{0:T(1024)}, s32[1024]{0:T(1024)S(1)}, u32[]{:S(2)}) copy-start(s32[1024]{0:T(1024)S(1)} %pad_clamp_fusion.1) | copy-start | bytes 12292
  10.5 7.5 %collective-permute-start = (bf16[4,2048]{1,0:T(4,128)(2,1)S(1)}, bf16[4,2048]{1,0:T(4,128)(2,1)S(1)}, u32[]{:S(2)}, u32[]{:S(2)}) collective-permute-start(bf16[4,2048]{1,0:T(4,128)(2,1)S(1)} %get-tuple-element.54), channel_id=1, source_target_pairs={{0,1},{1,2},{2,3},{3,4},{4,5},{5,6},{6,7},{7,8},{8,9},{9,10},{10,1... | collective-permute-start | bytes 49160 | tf_op jit(solution)/shard_map/ppermute | solution.py:16
  12.4 6.0 collective-permute-start.1
  17.9 43.5 %copy-start.69 = (pred[96]{0:T(512)(128)(4,1)}, pred[96]{0:T(512)(128)(4,1)S(1)}, u32[]{:S(2)}) copy-start(pred[96]{0:T(512)(128)(4,1)S(1)} %compare_and_fusion) | copy-start | bytes 292
  17.9 27.2 %copy-start.79 = (s32[1024]{0:T(1024)}, s32[1024]{0:T(1024)S(1)}, u32[]{:S(2)}) copy-start(s32[1024]{0:T(1024)S(1)} %pad_clamp_fusion) | copy-start | bytes 12292
  18.0 42.3 %copy-start.47 = (bf16[25]{0:T(256)(128)(2,1)}, bf16[25]{0:T(256)(128)(2,1)S(1)}, u32[]{:S(2)}) copy-start(bf16[25]{0:T(256)(128)(2,1)S(1)} %pad.91.clone) | copy-start | bytes 154
  22.6 6.5 collective-permute-start.2
  25.2 5.3 collective-permute-start.3
  37.1 6.5 collective-permute-start.4
  39.6 5.4 collective-permute-start.5
  51.0 9.3 %collective-permute-start.6 = (bf16[4,2048]{1,0:T(4,128)(2,1)S(1)}, bf16[4,2048]{1,0:T(4,128)(2,1)S(1)}, u32[]{:S(2)}, u32[]{:S(2)}) collective-permute-start(bf16[4,2048]{1,0:T(4,128)(2,1)S(1)} %get-tuple-element.48), channel_id=1, source_target_pairs={{0,1},{1,2},{2,3},{3,4},{4,5},{5,6},{6,7},{7,8},{8,9},{9,10},{10,1... | collective-permute-start | bytes 49160 | tf_op jit(solution)/shard_map/ppermute | solution.py:16
  53.5 6.8 %collective-permute-start.7 = (bf16[4,2048]{1,0:T(4,128)(2,1)S(1)}, bf16[4,2048]{1,0:T(4,128)(2,1)S(1)}, u32[]{:S(2)}, u32[]{:S(2)}) collective-permute-start(bf16[4,2048]{1,0:T(4,128)(2,1)S(1)} %get-tuple-element.49), channel_id=1, source_target_pairs={{1,0},{2,1},{3,2},{4,3},{5,4},{6,5},{7,6},{8,7},{9,8},{10,9},{11,1... | collective-permute-start | bytes 49160 | tf_op jit(solution)/shard_map/ppermute | solution.py:16
  66.7 109.6 %copy-start.64 = (pred[8]{0:T(512)(128)(4,1)S(1)}, pred[8]{0:T(512)(128)(4,1)}, u32[]{:S(2)}) copy-start(pred[8]{0:T(512)(128)(4,1)} %copy-done.63) | copy-start | bytes 28
  66.7 109.7 %copy-start.58 = (pred[2,4]{1,0:T(4,128)(4,1)S(1)}, pred[2,4]{1,0:T(4,128)(4,1)}, u32[]{:S(2)}) copy-start(pred[2,4]{1,0:T(4,128)(4,1)} %copy-done.57) | copy-start | bytes 28
  66.7 244.3 %all-reduce.7.cloned.1.call-start = ((), (), s32[]{:S(2)}) async-start(), calls=%async_computation.1 | async-start | bytes 131072 | tf_op jit(solution)/shard_map/psum | solution.py:49
  154.9 29.6 %copy-start.48 = (bf16[25]{0:T(256)(128)(2,1)S(1)}, bf16[25]{0:T(256)(128)(2,1)}, u32[]{:S(2)}) copy-start(bf16[25]{0:T(256)(128)(2,1)} %copy-done.47) | copy-start | bytes 154
  176.5 6.5 collective-permute-start.8
  178.5 6.0 collective-permute-start.9
  187.5 10.0 %copy-start.49 = (bf16[25]{0:T(256)(128)(2,1)S(1)}, bf16[25]{0:T(256)(128)(2,1)}, u32[]{:S(2)}) copy-start(bf16[25]{0:T(256)(128)(2,1)} %copy-done.47) | copy-start | bytes 154
  189.5 6.9 %collective-permute-start.10 = (bf16[4,2048]{1,0:T(4,128)(2,1)S(1)}, bf16[4,2048]{1,0:T(4,128)(2,1)S(1)}, u32[]{:S(2)}, u32[]{:S(2)}) collective-permute-start(bf16[4,2048]{1,0:T(4,128)(2,1)S(1)} %get-tuple-element.44), channel_id=1, source_target_pairs={{0,1},{1,2},{2,3},{3,4},{4,5},{5,6},{6,7},{7,8},{8,9},{9,10},{10,1... | collective-permute-start | bytes 49160 | tf_op jit(solution)/shard_map/ppermute | solution.py:16
  191.5 6.0 collective-permute-start.11
  204.0 11.5 %copy-start.27 = (f32[16,2048]{1,0:T(8,128)S(1)}, f32[16,2048]{1,0:T(8,128)}, u32[]{:S(2)}) copy-start(f32[16,2048]{1,0:T(8,128)} %get-tuple-element.22) | copy-start | bytes 393220
  207.1 10.4 %collective-permute-start.12 = (bf16[4,2048]{1,0:T(4,128)(2,1)}, bf16[4,2048]{1,0:T(4,128)(2,1)S(1)}, u32[]{:S(2)}, u32[]{:S(2)}) collective-permute-start(bf16[4,2048]{1,0:T(4,128)(2,1)} %get-tuple-element.42), channel_id=1, source_target_pairs={{0,1},{1,2},{2,3},{3,4},{4,5},{5,6},{6,7},{7,8},{8,9},{9,10},{10,1... | collective-permute-start | bytes 49160 | tf_op jit(solution)/shard_map/ppermute | solution.py:16
  209.0 8.4 %collective-permute-start.13 = (bf16[4,2048]{1,0:T(4,128)(2,1)S(1)}, bf16[4,2048]{1,0:T(4,128)(2,1)S(1)}, u32[]{:S(2)}, u32[]{:S(2)}) collective-permute-start(bf16[4,2048]{1,0:T(4,128)(2,1)S(1)} %get-tuple-element.43), channel_id=1, source_target_pairs={{1,0},{2,1},{3,2},{4,3},{5,4},{6,5},{7,6},{8,7},{9,8},{10,9},{11,1... | collective-permute-start | bytes 49160 | tf_op jit(solution)/shard_map/ppermute | solution.py:16
  224.7 109.1 %copy-start.66 = (pred[8]{0:T(512)(128)(4,1)S(1)}, pred[8]{0:T(512)(128)(4,1)}, u32[]{:S(2)}) copy-start(pred[8]{0:T(512)(128)(4,1)} %copy-done.63) | copy-start | bytes 28
  224.8 109.2 %copy-start.60 = (pred[2,4]{1,0:T(4,128)(4,1)S(1)}, pred[2,4]{1,0:T(4,128)(4,1)}, u32[]{:S(2)}) copy-start(pred[2,4]{1,0:T(4,128)(4,1)} %copy-done.57) | copy-start | bytes 28
  224.8 247.6 %all-reduce.9.cloned.1.call-start = ((), (), s32[]{:S(2)}) async-start(), calls=%async_computation.2 | async-start | bytes 131072 | tf_op jit(solution)/shard_map/psum | solution.py:49
  311.8 30.4 %copy-start.51 = (bf16[25]{0:T(256)(128)(2,1)S(1)}, bf16[25]{0:T(256)(128)(2,1)}, u32[]{:S(2)}) copy-start(bf16[25]{0:T(256)(128)(2,1)} %copy-done.47) | copy-start | bytes 154
  331.2 12.0 %copy-start.39 = (f32[96,32]{0,1:T(8,128)}, f32[96,32]{0,1:T(8,128)S(1)}, u32[]{:S(2)}) copy-start(f32[96,32]{0,1:T(8,128)S(1)} %fusion.94) | copy-start | bytes 36868
  334.1 6.6 collective-permute-start.14
  336.2 6.0 collective-permute-start.15
  347.6 10.9 %copy-start.52 = (bf16[25]{0:T(256)(128)(2,1)S(1)}, bf16[25]{0:T(256)(128)(2,1)}, u32[]{:S(2)}) copy-start(bf16[25]{0:T(256)(128)(2,1)} %copy-done.47) | copy-start | bytes 154
  350.7 6.5 collective-permute-start.16
  352.6 6.0 collective-permute-start.17
  364.1 11.7 %copy-start.4 = (f32[16,64,32]{1,2,0:T(8,128)S(1)}, f32[16,64,32]{1,2,0:T(8,128)}, u32[]{:S(2)}) copy-start(f32[16,64,32]{1,2,0:T(8,128)} %convolution_bitcast_fusion.5) | copy-start | bytes 393220
  365.2 10.9 %copy-start.28 = (f32[16,2048]{1,0:T(8,128)S(1)}, f32[16,2048]{1,0:T(8,128)}, u32[]{:S(2)}) copy-start(f32[16,2048]{1,0:T(8,128)} %get-tuple-element.18) | copy-start | bytes 393220
  368.2 10.7 %collective-permute-start.18 = (bf16[4,2048]{1,0:T(4,128)(2,1)}, bf16[4,2048]{1,0:T(4,128)(2,1)S(1)}, u32[]{:S(2)}, u32[]{:S(2)}) collective-permute-start(bf16[4,2048]{1,0:T(4,128)(2,1)} %get-tuple-element.36), channel_id=1, source_target_pairs={{0,1},{1,2},{2,3},{3,4},{4,5},{5,6},{6,7},{7,8},{8,9},{9,10},{10,1... | collective-permute-start | bytes 49160 | tf_op jit(solution)/shard_map/ppermute | solution.py:16
  370.2 8.8 %collective-permute-start.19 = (bf16[4,2048]{1,0:T(4,128)(2,1)S(1)}, bf16[4,2048]{1,0:T(4,128)(2,1)S(1)}, u32[]{:S(2)}, u32[]{:S(2)}) collective-permute-start(bf16[4,2048]{1,0:T(4,128)(2,1)S(1)} %get-tuple-element.37), channel_id=1, source_target_pairs={{1,0},{2,1},{3,2},{4,3},{5,4},{6,5},{7,6},{8,7},{9,8},{10,9},{11,1... | collective-permute-start | bytes 49160 | tf_op jit(solution)/shard_map/ppermute | solution.py:16
  385.0 109.0 %copy-start.6 = (f32[16,2048]{1,0:T(8,128)S(1)}, f32[16,2048]{1,0:T(8,128)}, u32[]{:S(2)}) copy-start(f32[16,2048]{1,0:T(8,128)} %get-tuple-element.9) | copy-start | bytes 393220
  386.2 108.6 %copy-start.68 = (pred[8]{0:T(512)(128)(4,1)S(1)}, pred[8]{0:T(512)(128)(4,1)}, u32[]{:S(2)}) copy-start(pred[8]{0:T(512)(128)(4,1)} %copy-done.63) | copy-start | bytes 28
  386.2 108.7 %copy-start.62 = (pred[2,4]{1,0:T(4,128)(4,1)S(1)}, pred[2,4]{1,0:T(4,128)(4,1)}, u32[]{:S(2)}) copy-start(pred[2,4]{1,0:T(4,128)(4,1)} %copy-done.57) | copy-start | bytes 28
  386.2 262.4 %all-reduce.11.cloned.1.call-start = ((), (), s32[]{:S(2)}) async-start(), calls=%async_computation.3 | async-start | bytes 131072 | tf_op jit(solution)/shard_map/psum | solution.py:49
  473.2 28.2 %copy-start.13 = (f32[1024,32]{0,1:T(8,128)S(1)}, f32[1024,32]{0,1:T(8,128)}, u32[]{:S(2)}) copy-start(f32[1024,32]{0,1:T(8,128)} %copy-done.12) | copy-start | bytes 393220
  492.7 9.8 %copy-start.41 = (f32[96,32]{0,1:T(8,128)}, f32[96,32]{0,1:T(8,128)S(1)}, u32[]{:S(2)}) copy-start(f32[96,32]{0,1:T(8,128)S(1)} %fusion.89) | copy-start | bytes 36868
  495.0 8.5 %collective-permute-start.20 = (bf16[4,2048]{1,0:T(4,128)(2,1)S(1)}, bf16[4,2048]{1,0:T(4,128)(2,1)S(1)}, u32[]{:S(2)}, u32[]{:S(2)}) collective-permute-start(bf16[4,2048]{1,0:T(4,128)(2,1)S(1)} %get-tuple-element.34), channel_id=1, source_target_pairs={{0,1},{1,2},{2,3},{3,4},{4,5},{5,6},{6,7},{7,8},{8,9},{9,10},{10,1... | collective-permute-start | bytes 49160 | tf_op jit(solution)/shard_map/ppermute | solution.py:16
  496.9 6.6 collective-permute-start.21
  509.0 12.9 %copy-start.9 = (f32[1024,32]{1,0:T(8,128)S(1)}, f32[1024,32]{1,0:T(8,128)}, u32[]{:S(2)}) copy-start(f32[1024,32]{1,0:T(8,128)} %copy.112) | copy-start | bytes 393220
  509.0 12.9 %copy-start.11 = (f32[1024,32]{1,0:T(8,128)S(1)}, f32[1024,32]{1,0:T(8,128)}, u32[]{:S(2)}) copy-start(f32[1024,32]{1,0:T(8,128)} %copy.113) | copy-start | bytes 393220
  513.5 11.9 %copy-start.16 = (f32[1024,32]{0,1:T(8,128)S(1)}, f32[1024,32]{0,1:T(8,128)}, u32[]{:S(2)}) copy-start(f32[1024,32]{0,1:T(8,128)} %reshape_reshape.26) | copy-start | bytes 393220
  515.0 12.4 %collective-permute-start.22 = (bf16[4,2048]{1,0:T(4,128)(2,1)S(1)}, bf16[4,2048]{1,0:T(4,128)(2,1)S(1)}, u32[]{:S(2)}, u32[]{:S(2)}) collective-permute-start(bf16[4,2048]{1,0:T(4,128)(2,1)S(1)} %get-tuple-element.32), channel_id=1, source_target_pairs={{0,1},{1,2},{2,3},{3,4},{4,5},{5,6},{6,7},{7,8},{8,9},{9,10},{10,1... | collective-permute-start | bytes 49160 | tf_op jit(solution)/shard_map/ppermute | solution.py:16
  516.9 10.5 %copy-start.55 = (bf16[25]{0:T(256)(128)(2,1)S(1)}, bf16[25]{0:T(256)(128)(2,1)}, u32[]{:S(2)}) copy-start(bf16[25]{0:T(256)(128)(2,1)} %copy-done.47) | copy-start | bytes 154
  517.0 10.5 %collective-permute-start.23 = (bf16[4,2048]{1,0:T(4,128)(2,1)S(1)}, bf16[4,2048]{1,0:T(4,128)(2,1)S(1)}, u32[]{:S(2)}, u32[]{:S(2)}) collective-permute-start(bf16[4,2048]{1,0:T(4,128)(2,1)S(1)} %get-tuple-element.33), channel_id=1, source_target_pairs={{1,0},{2,1},{3,2},{4,3},{5,4},{6,5},{7,6},{8,7},{9,8},{10,9},{11,1... | collective-permute-start | bytes 49160 | tf_op jit(solution)/shard_map/ppermute | solution.py:16
  531.6 12.0 %copy-start.8 = (f32[1024,32]{1,0:T(8,128)S(1)}, f32[1024,32]{1,0:T(8,128)}, u32[]{:S(2)}) copy-start(f32[1024,32]{1,0:T(8,128)} %copy.129) | copy-start | bytes 393220
  531.6 12.0 %copy-start.40 = (f32[96,32]{0,1:T(8,128)S(1)}, f32[96,32]{0,1:T(8,128)}, u32[]{:S(2)}) copy-start(f32[96,32]{0,1:T(8,128)} %copy-done.39) | copy-start | bytes 36868
  532.9 10.7 %copy-start.10 = (f32[1024,32]{1,0:T(8,128)S(1)}, f32[1024,32]{1,0:T(8,128)}, u32[]{:S(2)}) copy-start(f32[1024,32]{1,0:T(8,128)} %copy.130) | copy-start | bytes 393220
  537.1 15.1 %collective-permute-start.24 = (bf16[4,2048]{1,0:T(4,128)(2,1)}, bf16[4,2048]{1,0:T(4,128)(2,1)}, u32[]{:S(2)}, u32[]{:S(2)}) collective-permute-start(bf16[4,2048]{1,0:T(4,128)(2,1)} %get-tuple-element.30), channel_id=1, source_target_pairs={{0,1},{1,2},{2,3},{3,4},{4,5},{5,6},{6,7},{7,8},{8,9},{9,10},{10,1... | collective-permute-start | bytes 49160 | tf_op jit(solution)/shard_map/ppermute | solution.py:16
  539.1 13.2 %collective-permute-start.25 = (bf16[4,2048]{1,0:T(4,128)(2,1)}, bf16[4,2048]{1,0:T(4,128)(2,1)}, u32[]{:S(2)}, u32[]{:S(2)}) collective-permute-start(bf16[4,2048]{1,0:T(4,128)(2,1)} %get-tuple-element.31), channel_id=1, source_target_pairs={{1,0},{2,1},{3,2},{4,3},{5,4},{6,5},{7,6},{8,7},{9,8},{10,9},{11,1... | collective-permute-start | bytes 49160 | tf_op jit(solution)/shard_map/ppermute | solution.py:16
  563.1 105.7 %copy-start.25 = (f32[1024,32]{0,1:T(8,128)S(1)}, f32[1024,32]{0,1:T(8,128)}, u32[]{:S(2)}) copy-start(f32[1024,32]{0,1:T(8,128)} %copy.168) | copy-start | bytes 393220
  563.1 105.7 %copy-start.33 = (f32[1024,32]{0,1:T(8,128)S(1)}, f32[1024,32]{0,1:T(8,128)}, u32[]{:S(2)}) copy-start(f32[1024,32]{0,1:T(8,128)} %copy-done.32) | copy-start | bytes 393220
  563.1 105.7 %copy-start.35 = (f32[1024,32]{0,1:T(8,128)S(1)}, f32[1024,32]{0,1:T(8,128)}, u32[]{:S(2)}) copy-start(f32[1024,32]{0,1:T(8,128)} %copy-done.34) | copy-start | bytes 393220
  (46 other events, 137.9 us)
Sparse Core Ops, SparseCore 0:
  66.8 87.2 all-reduce.4
  224.9 86.0 all-reduce.6
  386.3 86.0 all-reduce.8
  562.5 86.0 all-reduce.10
where the time goes:
time: 688 us; the launch traced here: 680 us
  waiting for transfers between devices  350 us (51%)
  other arithmetic  104 us (15%)
  local copies, waits for them, and re-layouts  94.6 us (14%)
  starting transfers between devices  85.5 us (12%)
  matrix products  28.9 us (4%)
  between operations  16.5 us (2%)
    psum x4, waiting for transfers between devices, basis_sums(): total_sum = lax.psum(partial_sum, ('leaf', 'sub'))  342 us
    ppermute x26, starting transfers between devices, from_behind(): lax.ppermute(value, axis, [(source, source + steps) for source in range(f...  85.1 us
    another operation x12, other arithmetic, shards(): factor = jnp.linalg.cholesky(square_block)  37.9 us
    another operation x8, other arithmetic, shards(): coeffs = jax.scipy.linalg.cho_solve((factor, True), right_block)  32 us
    reshape x13, local copies, waits for them, and re-layouts, couple_apply(): jnp.take(extended, positions, axis=0).reshape(local_count, FACES * DOF, RHS)  27.4 us
  transfers between devices with their start and end apart: 30, of which 11 were waited for; matrix products, arithmetic and copies ran while one was open for 5% of the time, Pallas kernels for 0%

commit v1 on v0

--- a/solution.py
+++ b/solution.py
@@ -46,7 +46,8 @@
     partial_sum = jnp.dot(
         stacked.T, stacked, precision=lax.Precision.HIGHEST, preferred_element_type=jnp.float32
     )
-    total_sum = lax.psum(partial_sum, ("leaf", "sub"))
+    terms = lax.all_gather(partial_sum, ("leaf", "sub"))
+    total_sum = jnp.sum(terms, axis=0)
     return (total_sum[: SSTEP * RHS, : SSTEP * RHS], total_sum[: SSTEP * RHS, SSTEP * RHS :])
 
 

time: 688 us -> 476 us (0.69)
  the two profiles are of different devices: /device:TPU:8 before, /device:TPU:0 now
where the time goes in v1:
time: 476 us; the launch traced here: 467 us
  waiting for transfers between devices  169 us (36%)
  other arithmetic  101 us (21%)
  local copies, waits for them, and re-layouts  86.8 us (18%)
  starting transfers between devices  67.8 us (14%)
  matrix products  26.2 us (6%)
  between operations  16.4 us (3%)
    all_gather x4, waiting for transfers between devices, basis_sums(): terms = lax.all_gather(partial_sum, ('leaf', 'sub'))  153 us
    ppermute x26, starting transfers between devices, from_behind(): lax.ppermute(value, axis, [(source, source + steps) for source in range(f...  67.4 us
    another operation x12, other arithmetic, shards(): factor = jnp.linalg.cholesky(square_block)  37.9 us
    another operation x8, other arithmetic, shards(): coeffs = jax.scipy.linalg.cho_solve((factor, True), right_block)  32.1 us
    reshape x13, local copies, waits for them, and re-layouts, couple_apply(): jnp.take(extended, positions, axis=0).reshape(local_count, FACES * DOF, RHS)  26.4 us
    ppermute x26, waiting for transfers between devices, from_behind(): lax.ppermute(value, axis, [(source, source + steps) for source in range(f...  16.7 us
    dot_general x13, matrix products, couple_apply(): jnp.einsum('eik,ekr->eir', couple, gathered, preferred_element_type=jnp.f...  12.5 us
    gather x13, local copies, waits for them, and re-layouts, couple_apply(): jnp.take(extended, positions, axis=0).reshape(local_count, FACES * DOF, RHS)  12.3 us
  transfers between devices with their start and end apart: 30, of which 13 were waited for; matrix products, arithmetic and copies ran while one was open for 6% of the time, Pallas kernels for 0%

profile of v1, /device:TPU:0, one launch (start us, length us, event | category | flops | bytes accessed | tf_op | source)
XLA Modules:
  0.0 467.4 jit_solution(17120015142865215574)
XLA Ops:
  10.5 2.4 collective-permute-start
  12.9 1.3 collective-permute-start.1
  15.2 2.9 collective-permute-done.1
  20.4 1.3 convolution_bitcast_fusion.12
  24.0 4.4 collective-permute-start.2
  28.4 1.3 collective-permute-start.3
  29.7 1.8 collective-permute-done.3
  36.5 4.7 %collective-permute-start.4 = (bf16[4,2048]{1,0:T(4,128)(2,1)S(1)}, bf16[4,2048]{1,0:T(4,128)(2,1)S(1)}, u32[]{:S(2)}, u32[]{:S(2)}) collective-permute-start(bf16[4,2048]{1,0:T(4,128)(2,1)S(1)} %get-tuple-element.50), channel_id=1, source_target_pairs={{0,1},{1,2},{2,3},{3,4},{4,5},{5,6},{6,7},{7,8},{8,9},{9,10},{10,1... | collective-permute-start | bytes 49160 | tf_op jit(solution)/shard_map/ppermute | solution.py:16
  41.2 1.3 collective-permute-start.5
  42.5 1.8 collective-permute-done.5
  46.2 2.2 reshape.262
  48.4 1.3 fusion.132
  51.1 4.8 %collective-permute-start.6 = (bf16[4,2048]{1,0:T(4,128)(2,1)S(1)}, bf16[4,2048]{1,0:T(4,128)(2,1)S(1)}, u32[]{:S(2)}, u32[]{:S(2)}) collective-permute-start(bf16[4,2048]{1,0:T(4,128)(2,1)S(1)} %get-tuple-element.48), channel_id=1, source_target_pairs={{0,1},{1,2},{2,3},{3,4},{4,5},{5,6},{6,7},{7,8},{8,9},{9,10},{10,1... | collective-permute-start | bytes 49160 | tf_op jit(solution)/shard_map/ppermute | solution.py:16
  56.0 1.8 collective-permute-start.7
  62.9 2.2 reshape.265
  68.0 41.0 %all-gather.9.cloned.1.call-done = f32[2048,128]{1,0:T(8,128)} async-done(((f32[128,128]{1,0:T(8,128)}), f32[2048,128]{1,0:T(8,128)}) %all-gather.9.cloned.1.call-update) | async-done | bytes 1048592 | tf_op jit(solution)/shard_map/all_gather | solution.py:49
  109.0 1.3 reduce_sum.36
  110.5 8.8 %cholesky.74 = f32[96,96]{1,0:T(8,128)S(1)} custom-call(f32[96,96]{1,0:T(8,128)S(1)} %fusion.107), custom_call_target="Cholesky" | custom-call | tf_op jit(solution)/shard_map/jit(cholesky)/cholesky | solution.py:69
  120.6 7.4 %custom-call.10 = f32[1,96,96]{1,2,0:T(8,128)S(1)} custom-call(f32[1,96,96]{2,1,0:T(8,128)S(1)} %fusion.80), custom_call_target="InvertDiagBlocksLowerTriangular" | custom-call | tf_op jit(solution)/shard_map/jit(_cho_solve)/triangular_solve | solution.py:70
  130.7 2.2 collective-permute-start.8
  132.9 1.5 collective-permute-start.9
  134.4 1.6 collective-permute-done.9
  137.9 2.2 reshape.271
  142.8 4.2 collective-permute-start.10
  147.1 1.3 collective-permute-start.11
  148.4 1.8 collective-permute-done.11
  152.6 1.3 fusion.133
  155.3 4.6 collective-permute-start.12
  159.9 1.3 collective-permute-start.13
  167.1 2.2 reshape.277
  172.7 40.5 %all-gather.11.cloned.1.call-done = f32[2048,128]{1,0:T(8,128)} async-done(((f32[128,128]{1,0:T(8,128)}), f32[2048,128]{1,0:T(8,128)}) %all-gather.11.cloned.1.call-update) | async-done | bytes 1048592 | tf_op jit(solution)/shard_map/all_gather | solution.py:49
  214.6 8.8 %cholesky.85 = f32[96,96]{1,0:T(8,128)S(1)} custom-call(f32[96,96]{1,0:T(8,128)S(1)} %fusion.103), custom_call_target="Cholesky" | custom-call | tf_op jit(solution)/shard_map/jit(cholesky)/cholesky | solution.py:69
  224.8 7.4 %custom-call.11 = f32[1,96,96]{1,2,0:T(8,128)S(1)} custom-call(f32[1,96,96]{2,1,0:T(8,128)S(1)} %fusion.81), custom_call_target="InvertDiagBlocksLowerTriangular" | custom-call | tf_op jit(solution)/shard_map/jit(_cho_solve)/triangular_solve | solution.py:70
  235.5 2.2 collective-permute-start.14
  237.7 1.3 collective-permute-start.15
  239.0 1.8 collective-permute-done.15
  242.7 2.2 reshape.283
  249.3 4.2 collective-permute-start.16
  253.5 1.3 collective-permute-start.17
  254.8 1.8 collective-permute-done.17
  258.5 2.2 reshape.286
  260.8 1.3 fusion.134
  266.3 4.6 collective-permute-start.18
  271.0 1.7 collective-permute-start.19
  279.8 2.2 reshape.289
  285.2 40.7 %all-gather.13.cloned.1.call-done = f32[2048,128]{1,0:T(8,128)} async-done(((f32[128,128]{1,0:T(8,128)}), f32[2048,128]{1,0:T(8,128)}) %all-gather.13.cloned.1.call-update) | async-done | bytes 1048592 | tf_op jit(solution)/shard_map/all_gather | solution.py:49
  325.9 1.3 reduce_sum.38
  327.3 8.8 %cholesky.96 = f32[96,96]{1,0:T(8,128)S(1)} custom-call(f32[96,96]{1,0:T(8,128)S(1)} %fusion.99), custom_call_target="Cholesky" | custom-call | tf_op jit(solution)/shard_map/jit(cholesky)/cholesky | solution.py:69
  337.5 7.4 %custom-call.12 = f32[1,96,96]{1,2,0:T(8,128)S(1)} custom-call(f32[1,96,96]{2,1,0:T(8,128)S(1)} %fusion.82), custom_call_target="InvertDiagBlocksLowerTriangular" | custom-call | tf_op jit(solution)/shard_map/jit(_cho_solve)/triangular_solve | solution.py:70
  347.7 2.2 collective-permute-start.20
  349.8 1.5 collective-permute-start.21
  351.3 1.6 collective-permute-done.21
  354.8 2.2 reshape.295
  361.4 4.2 collective-permute-start.22
  365.6 1.3 collective-permute-start.23
  367.0 1.8 collective-permute-done.23
  370.7 2.2 reshape.298
  372.9 1.3 fusion.135
  378.4 4.6 collective-permute-start.24
  383.1 1.3 collective-permute-start.25
  391.2 2.4 reshape.301
  407.1 30.4 %all-gather.15.cloned.1.call-done = f32[2048,128]{1,0:T(8,128)} async-done(((f32[128,128]{1,0:T(8,128)}), f32[2048,128]{1,0:T(8,128)}) %all-gather.15.cloned.1.call-update) | async-done | bytes 1048592 | tf_op jit(solution)/shard_map/all_gather | solution.py:49
  439.0 8.8 %cholesky.107 = f32[96,96]{1,0:T(8,128)S(1)} custom-call(f32[96,96]{1,0:T(8,128)S(1)} %fusion.95), custom_call_target="Cholesky" | custom-call | tf_op jit(solution)/shard_map/jit(cholesky)/cholesky | solution.py:69
  449.1 7.4 %custom-call.13 = f32[1,96,96]{1,2,0:T(8,128)S(1)} custom-call(f32[1,96,96]{2,1,0:T(8,128)S(1)} %fusion.83), custom_call_target="InvertDiagBlocksLowerTriangular" | custom-call | tf_op jit(solution)/shard_map/jit(_cho_solve)/triangular_solve | solution.py:70
  (456 shorter events, 118.0 us)
Async XLA Ops:
  7.2 13.2 %copy-start = (bf16[16,64,384]{2,1,0:T(8,128)(2,1)S(1)}, bf16[16,64,384]{2,1,0:T(8,128)(2,1)}, u32[]{:S(2)}) copy-start(bf16[16,64,384]{2,1,0:T(8,128)(2,1)} %param.14) | copy-start | bytes 2359300
  7.2 101.8 %all-gather.9.cloned.1.call-start = ((), (), s32[]{:S(2)}) async-start(), calls=%async_computation | async-start | bytes 1114112 | tf_op jit(solution)/shard_map/all_gather | solution.py:49
  8.0 43.0 %copy-start.48 = (pred[2,4]{1,0:T(4,128)(4,1)}, pred[2,4]{1,0:T(4,128)(4,1)S(1)}, u32[]{:S(2)}) copy-start(pred[2,4]{1,0:T(4,128)(4,1)S(1)} %compare_bitcast_fusion) | copy-start | bytes 28
  8.8 42.2 %copy-start.65 = (pred[8]{0:T(512)(128)(4,1)}, pred[8]{0:T(512)(128)(4,1)S(1)}, u32[]{:S(2)}) copy-start(pred[8]{0:T(512)(128)(4,1)S(1)} %compare_and_fusion.1) | copy-start | bytes 28
  8.8 14.4 %copy-start.82 = (s32[1024]{0:T(1024)}, s32[1024]{0:T(1024)S(1)}, u32[]{:S(2)}) copy-start(s32[1024]{0:T(1024)S(1)} %pad_clamp_fusion.1) | copy-start | bytes 12292
  10.5 4.7 collective-permute-start
  12.9 5.2 %collective-permute-start.1 = (bf16[4,2048]{1,0:T(4,128)(2,1)S(1)}, bf16[4,2048]{1,0:T(4,128)(2,1)S(1)}, u32[]{:S(2)}, u32[]{:S(2)}) collective-permute-start(bf16[4,2048]{1,0:T(4,128)(2,1)S(1)} %get-tuple-element.55), channel_id=1, source_target_pairs={{1,0},{2,1},{3,2},{4,3},{5,4},{6,5},{7,6},{8,7},{9,8},{10,9},{11,1... | collective-permute-start | bytes 49160 | tf_op jit(solution)/shard_map/ppermute | solution.py:16
  15.0 47.0 %copy-start.72 = (pred[96]{0:T(512)(128)(4,1)}, pred[96]{0:T(512)(128)(4,1)S(1)}, u32[]{:S(2)}) copy-start(pred[96]{0:T(512)(128)(4,1)S(1)} %compare_and_fusion) | copy-start | bytes 292
  15.2 45.8 %copy-start.55 = (bf16[25]{0:T(256)(128)(2,1)}, bf16[25]{0:T(256)(128)(2,1)S(1)}, u32[]{:S(2)}) copy-start(bf16[25]{0:T(256)(128)(2,1)S(1)} %pad.91.clone) | copy-start | bytes 154
  23.2 34.6 %copy-start.11 = (f32[16,2048]{1,0:T(8,128)}, f32[16,2048]{1,0:T(8,128)S(1)}, u32[]{:S(2)}) copy-start(f32[16,2048]{1,0:T(8,128)S(1)} %get-tuple-element.13) | copy-start | bytes 393220
  24.0 5.7 %collective-permute-start.2 = (bf16[4,2048]{1,0:T(4,128)(2,1)S(1)}, bf16[4,2048]{1,0:T(4,128)(2,1)S(1)}, u32[]{:S(2)}, u32[]{:S(2)}) collective-permute-start(bf16[4,2048]{1,0:T(4,128)(2,1)S(1)} %get-tuple-element.52), channel_id=1, source_target_pairs={{0,1},{1,2},{2,3},{3,4},{4,5},{5,6},{6,7},{7,8},{8,9},{9,10},{10,1... | collective-permute-start | bytes 49160 | tf_op jit(solution)/shard_map/ppermute | solution.py:16
  28.4 3.1 collective-permute-start.3
  36.5 6.0 %collective-permute-start.4 = (bf16[4,2048]{1,0:T(4,128)(2,1)S(1)}, bf16[4,2048]{1,0:T(4,128)(2,1)S(1)}, u32[]{:S(2)}, u32[]{:S(2)}) collective-permute-start(bf16[4,2048]{1,0:T(4,128)(2,1)S(1)} %get-tuple-element.50), channel_id=1, source_target_pairs={{0,1},{1,2},{2,3},{3,4},{4,5},{5,6},{6,7},{7,8},{8,9},{9,10},{10,1... | collective-permute-start | bytes 49160 | tf_op jit(solution)/shard_map/ppermute | solution.py:16
  41.2 3.1 collective-permute-start.5
  49.9 9.1 %copy-start.31 = (f32[16,2048]{1,0:T(8,128)S(1)}, f32[16,2048]{1,0:T(8,128)}, u32[]{:S(2)}) copy-start(f32[16,2048]{1,0:T(8,128)} %get-tuple-element.26) | copy-start | bytes 393220
  51.1 9.9 %collective-permute-start.6 = (bf16[4,2048]{1,0:T(4,128)(2,1)S(1)}, bf16[4,2048]{1,0:T(4,128)(2,1)S(1)}, u32[]{:S(2)}, u32[]{:S(2)}) collective-permute-start(bf16[4,2048]{1,0:T(4,128)(2,1)S(1)} %get-tuple-element.48), channel_id=1, source_target_pairs={{0,1},{1,2},{2,3},{3,4},{4,5},{5,6},{6,7},{7,8},{8,9},{9,10},{10,1... | collective-permute-start | bytes 49160 | tf_op jit(solution)/shard_map/ppermute | solution.py:16
  56.0 5.0 %collective-permute-start.7 = (bf16[4,2048]{1,0:T(4,128)(2,1)S(1)}, bf16[4,2048]{1,0:T(4,128)(2,1)S(1)}, u32[]{:S(2)}, u32[]{:S(2)}) collective-permute-start(bf16[4,2048]{1,0:T(4,128)(2,1)S(1)} %get-tuple-element.49), channel_id=1, source_target_pairs={{1,0},{2,1},{3,2},{4,3},{5,4},{6,5},{7,6},{8,7},{9,8},{10,9},{11,1... | collective-permute-start | bytes 49160 | tf_op jit(solution)/shard_map/ppermute | solution.py:16
  67.9 145.3 %all-gather.11.cloned.1.call-start = ((), (), s32[]{:S(2)}) async-start(), calls=%async_computation.1 | async-start | bytes 1114112 | tf_op jit(solution)/shard_map/all_gather | solution.py:49
  109.0 20.7 %copy-start.12 = (f32[16,2048]{1,0:T(8,128)S(1)}, f32[16,2048]{1,0:T(8,128)}, u32[]{:S(2)}) copy-start(f32[16,2048]{1,0:T(8,128)} %copy-done.11) | copy-start | bytes 393220
  110.3 20.1 %copy-start.66 = (pred[8]{0:T(512)(128)(4,1)S(1)}, pred[8]{0:T(512)(128)(4,1)}, u32[]{:S(2)}) copy-start(pred[8]{0:T(512)(128)(4,1)} %copy-done.65) | copy-start | bytes 28
  110.3 20.2 %copy-start.49 = (pred[2,4]{1,0:T(4,128)(4,1)S(1)}, pred[2,4]{1,0:T(4,128)(4,1)}, u32[]{:S(2)}) copy-start(pred[2,4]{1,0:T(4,128)(4,1)} %copy-done.48) | copy-start | bytes 28
  110.5 25.5 %copy-start.56 = (bf16[25]{0:T(256)(128)(2,1)S(1)}, bf16[25]{0:T(256)(128)(2,1)}, u32[]{:S(2)}) copy-start(bf16[25]{0:T(256)(128)(2,1)} %copy-done.55) | copy-start | bytes 154
  130.7 3.6 collective-permute-start.8
  132.9 3.1 collective-permute-start.9
  140.7 7.7 %copy-start.6 = (f32[16,64,32]{1,2,0:T(8,128)}, f32[16,64,32]{1,2,0:T(8,128)S(1)}, u32[]{:S(2)}) copy-start(f32[16,64,32]{1,2,0:T(8,128)S(1)} %convolution_bitcast_fusion.8) | copy-start | bytes 393220
  140.8 9.4 %copy-start.57 = (bf16[25]{0:T(256)(128)(2,1)S(1)}, bf16[25]{0:T(256)(128)(2,1)}, u32[]{:S(2)}) copy-start(bf16[25]{0:T(256)(128)(2,1)} %copy-done.55) | copy-start | bytes 154
  142.8 5.6 %collective-permute-start.10 = (bf16[4,2048]{1,0:T(4,128)(2,1)S(1)}, bf16[4,2048]{1,0:T(4,128)(2,1)S(1)}, u32[]{:S(2)}, u32[]{:S(2)}) collective-permute-start(bf16[4,2048]{1,0:T(4,128)(2,1)S(1)} %get-tuple-element.44), channel_id=1, source_target_pairs={{0,1},{1,2},{2,3},{3,4},{4,5},{5,6},{6,7},{7,8},{8,9},{9,10},{10,1... | collective-permute-start | bytes 49160 | tf_op jit(solution)/shard_map/ppermute | solution.py:16
  147.1 3.1 collective-permute-start.11
  153.9 8.4 %copy-start.7 = (f32[16,64,32]{1,2,0:T(8,128)S(1)}, f32[16,64,32]{1,2,0:T(8,128)}, u32[]{:S(2)}) copy-start(f32[16,64,32]{1,2,0:T(8,128)} %copy-done.6) | copy-start | bytes 393220
  154.1 9.1 %copy-start.32 = (f32[16,2048]{1,0:T(8,128)S(1)}, f32[16,2048]{1,0:T(8,128)}, u32[]{:S(2)}) copy-start(f32[16,2048]{1,0:T(8,128)} %get-tuple-element.22) | copy-start | bytes 393220
  155.3 9.8 %collective-permute-start.12 = (bf16[4,2048]{1,0:T(4,128)(2,1)S(1)}, bf16[4,2048]{1,0:T(4,128)(2,1)S(1)}, u32[]{:S(2)}, u32[]{:S(2)}) collective-permute-start(bf16[4,2048]{1,0:T(4,128)(2,1)S(1)} %get-tuple-element.42), channel_id=1, source_target_pairs={{0,1},{1,2},{2,3},{3,4},{4,5},{5,6},{6,7},{7,8},{8,9},{9,10},{10,1... | collective-permute-start | bytes 49160 | tf_op jit(solution)/shard_map/ppermute | solution.py:16
  159.9 5.2 %collective-permute-start.13 = (bf16[4,2048]{1,0:T(4,128)(2,1)S(1)}, bf16[4,2048]{1,0:T(4,128)(2,1)S(1)}, u32[]{:S(2)}, u32[]{:S(2)}) collective-permute-start(bf16[4,2048]{1,0:T(4,128)(2,1)S(1)} %get-tuple-element.43), channel_id=1, source_target_pairs={{1,0},{2,1},{3,2},{4,3},{5,4},{6,5},{7,6},{8,7},{9,8},{10,9},{11,1... | collective-permute-start | bytes 49160 | tf_op jit(solution)/shard_map/ppermute | solution.py:16
  172.5 153.4 %all-gather.13.cloned.1.call-start = ((), (), s32[]{:S(2)}) async-start(), calls=%async_computation.2 | async-start | bytes 1114112 | tf_op jit(solution)/shard_map/all_gather | solution.py:49
  214.5 20.8 %copy-start.68 = (pred[8]{0:T(512)(128)(4,1)S(1)}, pred[8]{0:T(512)(128)(4,1)}, u32[]{:S(2)}) copy-start(pred[8]{0:T(512)(128)(4,1)} %copy-done.65) | copy-start | bytes 28
  214.5 20.9 %copy-start.51 = (pred[2,4]{1,0:T(4,128)(4,1)S(1)}, pred[2,4]{1,0:T(4,128)(4,1)}, u32[]{:S(2)}) copy-start(pred[2,4]{1,0:T(4,128)(4,1)} %copy-done.48) | copy-start | bytes 28
  214.6 26.2 %copy-start.59 = (bf16[25]{0:T(256)(128)(2,1)S(1)}, bf16[25]{0:T(256)(128)(2,1)}, u32[]{:S(2)}) copy-start(bf16[25]{0:T(256)(128)(2,1)} %copy-done.55) | copy-start | bytes 154
  232.6 9.2 %copy-start.39 = (f32[96,32]{0,1:T(8,128)}, f32[96,32]{0,1:T(8,128)S(1)}, u32[]{:S(2)}) copy-start(f32[96,32]{0,1:T(8,128)S(1)} %fusion.100) | copy-start | bytes 36868
  235.5 3.5 collective-permute-start.14
  237.7 3.1 collective-permute-start.15
  246.2 10.4 %copy-start.60 = (bf16[25]{0:T(256)(128)(2,1)S(1)}, bf16[25]{0:T(256)(128)(2,1)}, u32[]{:S(2)}) copy-start(bf16[25]{0:T(256)(128)(2,1)} %copy-done.55) | copy-start | bytes 154
  249.3 5.6 %collective-permute-start.16 = (bf16[4,2048]{1,0:T(4,128)(2,1)S(1)}, bf16[4,2048]{1,0:T(4,128)(2,1)S(1)}, u32[]{:S(2)}, u32[]{:S(2)}) collective-permute-start(bf16[4,2048]{1,0:T(4,128)(2,1)S(1)} %get-tuple-element.38), channel_id=1, source_target_pairs={{0,1},{1,2},{2,3},{3,4},{4,5},{5,6},{6,7},{7,8},{8,9},{9,10},{10,1... | collective-permute-start | bytes 49160 | tf_op jit(solution)/shard_map/ppermute | solution.py:16
  253.5 3.1 collective-permute-start.17
  262.1 11.6 %copy-start.8 = (f32[16,64,32]{1,2,0:T(8,128)S(1)}, f32[16,64,32]{1,2,0:T(8,128)}, u32[]{:S(2)}) copy-start(f32[16,64,32]{1,2,0:T(8,128)} %convolution_bitcast_fusion.5) | copy-start | bytes 393220
  266.3 11.5 %collective-permute-start.18 = (bf16[4,2048]{1,0:T(4,128)(2,1)}, bf16[4,2048]{1,0:T(4,128)(2,1)S(1)}, u32[]{:S(2)}, u32[]{:S(2)}) collective-permute-start(bf16[4,2048]{1,0:T(4,128)(2,1)} %get-tuple-element.36), channel_id=1, source_target_pairs={{0,1},{1,2},{2,3},{3,4},{4,5},{5,6},{6,7},{7,8},{8,9},{9,10},{10,1... | collective-permute-start | bytes 49160 | tf_op jit(solution)/shard_map/ppermute | solution.py:16
  271.0 6.9 %collective-permute-start.19 = (bf16[4,2048]{1,0:T(4,128)(2,1)S(1)}, bf16[4,2048]{1,0:T(4,128)(2,1)S(1)}, u32[]{:S(2)}, u32[]{:S(2)}) collective-permute-start(bf16[4,2048]{1,0:T(4,128)(2,1)S(1)} %get-tuple-element.37), channel_id=1, source_target_pairs={{1,0},{2,1},{3,2},{4,3},{5,4},{6,5},{7,6},{8,7},{9,8},{10,9},{11,1... | collective-permute-start | bytes 49160 | tf_op jit(solution)/shard_map/ppermute | solution.py:16
  274.0 8.9 %copy-start.17 = (f32[1024,32]{0,1:T(8,128)}, f32[1024,32]{0,1:T(8,128)S(1)}, u32[]{:S(2)}) copy-start(f32[1024,32]{0,1:T(8,128)S(1)} %reshape_reshape.28) | copy-start | bytes 393220
  285.1 152.4 %all-gather.15.cloned.1.call-start = ((), (), s32[]{:S(2)}) async-start(), calls=%async_computation.3 | async-start | bytes 1114112 | tf_op jit(solution)/shard_map/all_gather | solution.py:49
  325.8 20.8 %copy-start.10 = (f32[16,2048]{1,0:T(8,128)S(1)}, f32[16,2048]{1,0:T(8,128)}, u32[]{:S(2)}) copy-start(f32[16,2048]{1,0:T(8,128)} %get-tuple-element.9) | copy-start | bytes 393220
  327.2 20.2 %copy-start.70 = (pred[8]{0:T(512)(128)(4,1)S(1)}, pred[8]{0:T(512)(128)(4,1)}, u32[]{:S(2)}) copy-start(pred[8]{0:T(512)(128)(4,1)} %copy-done.65) | copy-start | bytes 28
  327.2 20.3 %copy-start.53 = (pred[2,4]{1,0:T(4,128)(4,1)S(1)}, pred[2,4]{1,0:T(4,128)(4,1)}, u32[]{:S(2)}) copy-start(pred[2,4]{1,0:T(4,128)(4,1)} %copy-done.48) | copy-start | bytes 28
  327.3 25.6 %copy-start.62 = (bf16[25]{0:T(256)(128)(2,1)S(1)}, bf16[25]{0:T(256)(128)(2,1)}, u32[]{:S(2)}) copy-start(bf16[25]{0:T(256)(128)(2,1)} %copy-done.55) | copy-start | bytes 154
  347.7 3.6 collective-permute-start.20
  349.8 3.1 collective-permute-start.21
  358.4 10.4 %copy-start.63 = (bf16[25]{0:T(256)(128)(2,1)S(1)}, bf16[25]{0:T(256)(128)(2,1)}, u32[]{:S(2)}) copy-start(bf16[25]{0:T(256)(128)(2,1)} %copy-done.55) | copy-start | bytes 154
  361.4 5.6 %collective-permute-start.22 = (bf16[4,2048]{1,0:T(4,128)(2,1)S(1)}, bf16[4,2048]{1,0:T(4,128)(2,1)S(1)}, u32[]{:S(2)}, u32[]{:S(2)}) collective-permute-start(bf16[4,2048]{1,0:T(4,128)(2,1)S(1)} %get-tuple-element.32), channel_id=1, source_target_pairs={{0,1},{1,2},{2,3},{3,4},{4,5},{5,6},{6,7},{7,8},{8,9},{9,10},{10,1... | collective-permute-start | bytes 49160 | tf_op jit(solution)/shard_map/ppermute | solution.py:16
  365.6 3.1 collective-permute-start.23
  374.2 11.2 %copy-start.5 = (f32[16,64,32]{1,2,0:T(8,128)S(1)}, f32[16,64,32]{1,2,0:T(8,128)}, u32[]{:S(2)}) copy-start(f32[16,64,32]{1,2,0:T(8,128)} %convolution_bitcast_fusion.2) | copy-start | bytes 393220
  375.3 11.0 %copy-start.30 = (f32[16,2048]{1,0:T(8,128)S(1)}, f32[16,2048]{1,0:T(8,128)}, u32[]{:S(2)}) copy-start(f32[16,2048]{1,0:T(8,128)} %get-tuple-element.14) | copy-start | bytes 393220
  378.4 10.8 %collective-permute-start.24 = (bf16[4,2048]{1,0:T(4,128)(2,1)}, bf16[4,2048]{1,0:T(4,128)(2,1)S(1)}, u32[]{:S(2)}, u32[]{:S(2)}) collective-permute-start(bf16[4,2048]{1,0:T(4,128)(2,1)} %get-tuple-element.30), channel_id=1, source_target_pairs={{0,1},{1,2},{2,3},{3,4},{4,5},{5,6},{6,7},{7,8},{8,9},{9,10},{10,1... | collective-permute-start | bytes 49160 | tf_op jit(solution)/shard_map/ppermute | solution.py:16
  383.1 6.2 %collective-permute-start.25 = (bf16[4,2048]{1,0:T(4,128)(2,1)S(1)}, bf16[4,2048]{1,0:T(4,128)(2,1)S(1)}, u32[]{:S(2)}, u32[]{:S(2)}) collective-permute-start(bf16[4,2048]{1,0:T(4,128)(2,1)S(1)} %get-tuple-element.31), channel_id=1, source_target_pairs={{1,0},{2,1},{3,2},{4,3},{5,4},{6,5},{7,6},{8,7},{9,8},{10,9},{11,1... | collective-permute-start | bytes 49160 | tf_op jit(solution)/shard_map/ppermute | solution.py:16
  406.7 50.3 %copy-start.25 = (f32[1024,32]{0,1:T(8,128)S(1)}, f32[1024,32]{0,1:T(8,128)}, u32[]{:S(2)}) copy-start(f32[1024,32]{0,1:T(8,128)} %copy.235) | copy-start | bytes 393220
  406.7 50.3 %copy-start.27 = (f32[1024,32]{0,1:T(8,128)S(1)}, f32[1024,32]{0,1:T(8,128)}, u32[]{:S(2)}) copy-start(f32[1024,32]{0,1:T(8,128)} %copy-done.26) | copy-start | bytes 393220
  406.9 50.1 %copy-start.29 = (f32[1024,32]{0,1:T(8,128)S(1)}, f32[1024,32]{0,1:T(8,128)}, u32[]{:S(2)}) copy-start(f32[1024,32]{0,1:T(8,128)} %copy-done.28) | copy-start | bytes 393220
  406.9 51.1 %copy-start.4 = (f32[1024,32]{1,0:T(8,128)S(1)}, f32[1024,32]{1,0:T(8,128)}, u32[]{:S(2)}) copy-start(f32[1024,32]{1,0:T(8,128)} %copy-done.3) | copy-start | bytes 393220
  (50 other events, 106.3 us)
Sparse Core Ops, SparseCore 0:
  68.1 40.9 all-gather.8
  172.6 40.5 all-gather.10
  285.2 40.5 all-gather.12
  396.9 40.5 all-gather.14
